TPU v7x, 32 devices: a whole 2x2x4 slice. The times are simulated.
32 devices in a mesh: parts: 2 (over y), blk: 4 (over z), win: 2 (over x), frq: 2 (over core).
Axes of the slice: x: 2, y: 2, z: 4, core: 2. Of those that a mesh axis runs over, the one named last changes fastest.
Arguments:
- traces: bfloat16 [2048, 4, 2048], P(('parts', 'blk'), 'win'), parts along dimension 0, may hold values from -48 to 48
- block_members: int32 [32, 64], P(('parts', 'blk')), parts along dimension 0, may hold values from 0 to 1023, as said below
- pair_blocks: int32 [16, 2], P('parts'), parts along dimension 0, may hold values from 0 to 15, as said below
- pair_owner: int32 [16, 1], P('parts'), parts along dimension 0, may hold values from 0 to 3, as said below
Outputs:
- coherency: bfloat16 [2, 32, 64, 64, 512], P(None, ('parts', 'blk'), 'win', None, 'frq'), parts along dimension 1
There are 2 independent parts, one for each index of `parts`. A program takes and returns all parts, laid end to end along the dimension named above; each array names one. Nothing has to cross between parts.
Inputs may be any that keep to these rules, and one draw needn't show every extreme that they name: `block_members`: row b holds the 64 stations of block b, all among the stations b // 4 * 4 * 64 to b // 4 * 4 * 64 + 4 * 64 - 1; every station lies in exactly one block. `pair_blocks`: row p is a pair (a, b) with a // 4 == p // 2 and a <= b <= a + 3; no pair appears twice; in each aligned group of 2 rows but the last, some pair has b among the next group's blocks. `pair_owner`: within each aligned group of 2 rows no owner is named twice; no owner is named more than 4 times in all, and some owner exactly 4 times; every owner is named.
All inputs are finite; a program needn't handle non-finite values.
Results may differ from a plain program's by a relative error of at most 0.0077.
Values may be sent and summed in bfloat16 or wider, within the bound.
A program may use at most 128 MiB of HBM per device.

v0:
```python
import functools
import math

import jax
import jax.numpy as jnp
import numpy as np
from jax import lax
from jax.experimental import pallas as pl
from jax.experimental.pallas import tpu as pltpu
from jax.sharding import PartitionSpec as P

FREQS = 512
PAIR_DEV = 2

eps_time = 1e-05
eps_power = 1e-06
MIB = 1024 * 1024


def dft_tables(samples, parts):
    bins_dev = FREQS // parts
    t = np.arange(samples, dtype=np.int64)[:, None]
    k = np.arange(1, FREQS + 1, dtype=np.int64)[None, :]
    angles = (t * k % samples).astype(np.float32) * np.float32(2.0 * math.pi / samples)
    cos = np.cos(angles.astype(np.float64)).reshape(samples, parts, bins_dev)
    sin = np.sin(angles.astype(np.float64)).reshape(samples, parts, bins_dev)
    table = np.concatenate([cos, -sin], axis=2).transpose(1, 0, 2)
    return table.astype(np.float32).astype(jnp.bfloat16)


def spectra_kernel(
    meta_ref, blocks_ref, owner_ref, members_ref, x_ref, table_ref,
    spill, first_send, second_local, mask, pick, spectra, perm, *, row_tile, win_dev,
):
    step = pl.program_id(0)
    block_count, width = members_ref.shape
    owners, nwin, first_rows, bins = first_send.shape
    pairs_dev = spill.shape[0]
    slots = pick.shape[0] // 2
    x = x_ref[...].astype(jnp.float32)
    centre = x - jnp.mean(x, axis=1, keepdims=True)
    spread = jnp.mean(centre * centre, axis=1, keepdims=True)
    normal = (centre * lax.rsqrt(spread + eps_time)).astype(jnp.bfloat16)
    product = jnp.dot(normal, table_ref[0], preferred_element_type=jnp.float32)
    start = pl.multiple_of(step * row_tile, row_tile)
    spectra[pl.ds(start, row_tile), :] = product.astype(jnp.bfloat16)

    @pl.when(step == pl.num_programs(0) - 1)
    def _():
        me = meta_ref[0]
        rows = spectra.shape[0]
        chunk = win_dev * width
        half = width // nwin
        local = members_ref[...] % (rows // win_dev) * win_dev
        place = jnp.concatenate([local + w for w in range(win_dev)], axis=1)
        for block in range(block_count):
            row = lax.broadcasted_iota(jnp.int32, (rows, chunk), 0)
            onehot = jnp.where(row == place[block : block + 1, :], 1.0, 0.0).astype(jnp.bfloat16)
            perm[block] = lax.dot_general(
                onehot, spectra[...], (((0,), (0,)), ((), ())), preferred_element_type=jnp.float32
            ).astype(jnp.bfloat16)

        def whole_block(out, n, block):
            inside = (block >= 0) & (block < block_count)

            @pl.when(inside)
            def _():
                for part in range(2):
                    out[n, part * chunk : part * chunk + chunk, :] = perm[
                        block, :, part * bins : part * bins + bins
                    ]

            @pl.when(jnp.logical_not(inside))
            def _():
                out[n] = jnp.zeros(out.shape[1:], out.dtype)

        def halves(n, block):
            @pl.when(block >= 0)
            def _():
                for h in range(nwin):
                    for part in range(2):
                        for w in range(win_dev):
                            at = (part * win_dev + w) * half
                            first_send[n, h, at : at + half, :] = perm[
                                block,
                                w * width + h * half : w * width + h * half + half,
                                part * bins : part * bins + bins,
                            ]

            @pl.when(block < 0)
            def _():
                first_send[n] = jnp.zeros(first_send.shape[1:], first_send.dtype)

        before = jnp.maximum(me - 1, 0) * pairs_dev
        for q in range(pairs_dev):
            whole_block(spill, q, blocks_ref[(before + q) * 2 + 1] - me * block_count)

        def to_owner(o, carry):
            first, second = jnp.int32(-1), jnp.int32(-1)
            for q in range(pairs_dev):
                pair = me * pairs_dev + q
                hit = owner_ref[pair] == o
                first_end = blocks_ref[2 * pair] - me * block_count
                second_end = blocks_ref[2 * pair + 1] - me * block_count
                first = jnp.where(hit, first_end, first)
                second = jnp.where(hit, second_end, second)
                value = jnp.where(hit & (second_end >= block_count), 1.0, 0.0)
                mask[o, q : q + 1, :] = jnp.full((1, bins), value, jnp.float32)
            halves(o, first)
            whole_block(second_local, o, second)
            return carry

        lax.fori_loop(0, owners, to_owner, 0)

        for n in range(2 * slots):
            pick[n] = 0

        def from_group(g, rank):
            hit = owner_ref[g * pairs_dev] == me
            for q in range(1, pairs_dev):
                hit = hit | (owner_ref[g * pairs_dev + q] == me)

            @pl.when(hit & (rank < slots))
            def _():
                pick[rank] = g
                pick[slots + rank] = 1

            return rank + hit.astype(jnp.int32)

        lax.fori_loop(0, owners, from_group, jnp.int32(0))


def spectra(meta, pair_blocks, pair_owner, members, x, table, owners, nwin, win_dev, slots):
    rows, samples = x.shape
    cols = table.shape[2]
    bins = cols // 2
    block_count, width = members.shape
    chunk = win_dev * width
    row_tile = rows // 2
    whole = 2 * chunk
    shapes = [
        jax.ShapeDtypeStruct((PAIR_DEV, whole, bins), jnp.bfloat16),
        jax.ShapeDtypeStruct((owners, nwin, whole // nwin, bins), jnp.bfloat16),
        jax.ShapeDtypeStruct((owners, whole, bins), jnp.bfloat16),
        jax.ShapeDtypeStruct((owners, PAIR_DEV, bins), jnp.float32),
        jax.ShapeDtypeStruct((2 * slots,), jnp.int32),
    ]

    def fixed(shape):
        return pl.BlockSpec(shape, lambda i, *_: (0,) * len(shape))

    return pl.pallas_call(
        functools.partial(spectra_kernel, row_tile=row_tile, win_dev=win_dev),
        grid_spec=pltpu.PrefetchScalarGridSpec(
            num_scalar_prefetch=3,
            grid=(rows // row_tile,),
            in_specs=[
                fixed(members.shape),
                pl.BlockSpec((row_tile, samples), lambda i, *_: (i, 0)),
                pl.BlockSpec((1, samples, cols), lambda i, m, *_: (m[1], 0, 0)),
            ],
            out_specs=[fixed(s.shape) for s in shapes[:-1]]
            + [pl.BlockSpec(memory_space=pltpu.SMEM)],
            scratch_shapes=[
                pltpu.VMEM((rows, cols), jnp.bfloat16),
                pltpu.VMEM((block_count, chunk, cols), jnp.bfloat16),
            ],
        ),
        out_shape=shapes,
        compiler_params=pltpu.CompilerParams(vmem_limit_bytes=48 * MIB),
        cost_estimate=pl.CostEstimate(
            flops=2 * rows * samples * cols, bytes_accessed=8 * MIB, transcendentals=rows
        ),
    )(meta, pair_blocks, pair_owner, members, x, table)


def exchange_kernel(
    n, nwin, spill, first_send, second_local, mask,
    first_out, second_out, first_x, second_x,
    spill_in, second_send,
    spill_sems, zf_send, zf_recv, zs_send, zs_recv, xf_send, xf_recv, xs_send, xs_recv, own_sems,
):
    me = lax.axis_index("blk")
    my_win = lax.axis_index("win")
    pairs_dev = spill.shape[0]

    def along(d):
        return {"blk": lax.rem(me + d, n)}

    def across(shift):
        return {"win": lax.rem(my_win + shift, nwin)}

    def remote(src, dst, send, recv, device):
        return pltpu.make_async_remote_copy(
            src_ref=src, dst_ref=dst, send_sem=send, recv_sem=recv,
            device_id=device, device_id_type=pl.DeviceIdType.MESH,
        )

    barrier = pltpu.get_barrier_semaphore()
    for d in range(1, n):
        pl.semaphore_signal(barrier, inc=1, device_id=along(d), device_id_type=pl.DeviceIdType.MESH)
    for s in range(1, nwin):
        pl.semaphore_signal(barrier, inc=1, device_id=across(s), device_id_type=pl.DeviceIdType.MESH)
    pl.semaphore_wait(barrier, n + nwin - 2)

    to_left = remote(spill, spill_in, spill_sems.at[0], spill_sems.at[1], along(n - 1))

    @pl.when(me > 0)
    def _():
        to_left.start()

    def first_to(d):
        return remote(
            first_send.at[lax.rem(me + d, n)], first_out.at[me], zf_send.at[d], zf_recv.at[d], along(d)
        )

    def second_to(d):
        return remote(
            second_send.at[lax.rem(me + d, n)], second_out.at[me], zs_send.at[d], zs_recv.at[d], along(d)
        )

    def first_across(d, shift):
        source = lax.rem(me + n - d, n)
        other = lax.rem(my_win + shift, nwin)
        ref = first_send if d == 0 else first_out
        k = d * nwin + shift
        return remote(
            ref.at[source, other], first_x.at[shift - 1, source], xf_send.at[k], xf_recv.at[k], across(shift)
        )

    def second_across(d, shift):
        source = lax.rem(me + n - d, n)
        ref = second_send if d == 0 else second_out
        k = d * nwin + shift
        return remote(
            ref.at[source], second_x.at[shift - 1, source], xs_send.at[k], xs_recv.at[k], across(shift)
        )

    order = sorted(range(1, n), key=lambda d: min(d, n - d))
    for d in order:
        first_to(d).start()
    own_first = pltpu.make_async_copy(first_send.at[me], first_out.at[me], own_sems.at[0])
    own_first.start()
    for shift in range(1, nwin):
        first_across(0, shift).start()

    @pl.when(me == n - 1)
    def _():
        spill_in[...] = jnp.zeros_like(spill_in)

    @pl.when(me < n - 1)
    def _():
        to_left.wait_recv()

    for d in order + [0]:
        o = lax.rem(me + d, n)
        total = second_local[o].astype(jnp.float32)
        for q in range(pairs_dev):
            total = total + spill_in[q].astype(jnp.float32) * mask[o, q : q + 1, :]
        second_send[o] = total.astype(jnp.bfloat16)
        if d:
            second_to(d).start()
    own_second = pltpu.make_async_copy(second_send.at[me], second_out.at[me], own_sems.at[1])
    own_second.start()
    for shift in range(1, nwin):
        second_across(0, shift).start()

    for d in order:
        first_to(d).wait_recv()
        for shift in range(1, nwin):
            first_across(d, shift).start()
    for d in order:
        second_to(d).wait_recv()
        for shift in range(1, nwin):
            second_across(d, shift).start()
    own_first.wait()
    own_second.wait()

    @pl.when(me > 0)
    def _():
        to_left.wait_send()

    for d in order:
        first_to(d).wait_send()
        second_to(d).wait_send()
    for d in range(n):
        for shift in range(1, nwin):
            first_across(d, shift).wait()
            second_across(d, shift).wait()


def exchange(spill, first_send, second_local, mask):
    n, nwin, first_rows, bins = first_send.shape
    rows = second_local.shape[1]
    hbm = pl.BlockSpec(memory_space=pl.ANY)
    vmem = pl.BlockSpec(memory_space=pltpu.VMEM)
    dma = pltpu.SemaphoreType.DMA
    sent = jax.ShapeDtypeStruct
    return pl.pallas_call(
        functools.partial(exchange_kernel, n, nwin),
        in_specs=[hbm, hbm, vmem, vmem],
        out_specs=[hbm] * 4,
        out_shape=[
            sent(first_send.shape, jnp.bfloat16),
            sent(second_local.shape, jnp.bfloat16),
            sent((nwin - 1, n, first_rows, bins), jnp.bfloat16),
            sent((nwin - 1, n, rows, bins), jnp.bfloat16),
        ],
        scratch_shapes=[
            pltpu.VMEM(spill.shape, jnp.bfloat16),
            pltpu.VMEM(second_local.shape, jnp.bfloat16),
            dma((2,)),
            dma((n,)), dma((n,)), dma((n,)), dma((n,)),
            dma((n * nwin,)), dma((n * nwin,)), dma((n * nwin,)), dma((n * nwin,)),
            dma((2,)),
        ],
        compiler_params=pltpu.CompilerParams(
            collective_id=0, has_side_effects=True, vmem_limit_bytes=32 * MIB
        ),
        cost_estimate=pl.CostEstimate(flops=0, bytes_accessed=4 * MIB, transcendentals=0),
    )(spill, first_send, second_local, mask)


def tiles_kernel(meta_ref, pick_ref, *refs, nwin, win_dev, first_rows, width):
    firsts, seconds = refs[:nwin], refs[nwin : 2 * nwin]
    out_ref, left, right = refs[2 * nwin :]
    slots = pl.num_programs(0)
    slot = pl.program_id(0)
    windows = nwin * win_dev
    bins = out_ref.shape[4]
    filled = pick_ref[slots + slot]

    @pl.when(filled == 0)
    def _():
        out_ref[...] = jnp.zeros_like(out_ref)

    @pl.when(filled != 0)
    def _():
        def whitened(ends, rows, scale):
            real, imag = [], []
            for ref in ends:
                view = ref[...].reshape(2, win_dev, rows, bins).astype(jnp.float32)
                for w in range(win_dev):
                    real.append(view[0, w])
                    imag.append(view[1, w])
            power = sum(r * r + i * i for r, i in zip(real, imag)) * (1.0 / windows)
            gain = lax.rsqrt(power + eps_power) * scale
            return [r * gain for r in real], [i * gain for i in imag]

        real, imag = whitened(firsts, first_rows, 1.0 / windows)
        for w in range(windows):
            for term, value in enumerate((real[w] + imag[w], real[w], imag[w])):
                for part in range(bins // 128):
                    left[part, term * windows + w] = value[:, part * 128 : part * 128 + 128]
        real, imag = whitened(seconds, width, 1.0)
        for w in range(windows):
            right[w] = real[w]
            right[windows + w] = real[w] + imag[w]
            right[2 * windows + w] = real[w] - imag[w]

        tile = 16
        for lane in range(0, bins, 128):

            def columns(t, carry, lane=lane):
                start = pl.multiple_of(t * tile, tile)
                held = [
                    right[n, pl.ds(start, tile), lane : lane + 128] for n in range(3 * windows)
                ]

                def row(i, c):
                    total = []
                    for term in range(3):
                        acc = None
                        for w in range(windows):
                            n = term * windows + w
                            one = left[lane // 128, n, pl.ds(i, 1), :]
                            prod = jnp.broadcast_to(one, (tile, 128)) * held[n]
                            acc = prod if acc is None else acc + prod
                        total.append(acc)
                    out_ref[0, 0, i, pl.ds(start, tile), lane : lane + 128] = (
                        total[0] - total[2]
                    ).astype(jnp.bfloat16)
                    out_ref[1, 0, i, pl.ds(start, tile), lane : lane + 128] = (
                        total[0] - total[1]
                    ).astype(jnp.bfloat16)
                    return c

                lax.fori_loop(0, first_rows, row, 0, unroll=8)
                return carry

            lax.fori_loop(0, width // tile, columns, 0)


def tiles(meta, pick, first_in, second_in, first_x, second_x, slots, win_dev, width):
    nwin, first_in_rows, bins = first_in.shape[1:]
    first_rows = first_in_rows // (2 * win_dev)
    whole = second_in.shape[1]
    shape = (2, slots, first_rows, width, bins)
    first_specs = [
        pl.BlockSpec((1, 1, first_in_rows, bins), lambda s, m, p: (p[s], m[2], 0, 0))
    ] + [
        pl.BlockSpec((1, 1, first_in_rows, bins), lambda s, m, p, k=k: (k, p[s], 0, 0))
        for k in range(nwin - 1)
    ]
    second_specs = [pl.BlockSpec((1, whole, bins), lambda s, m, p: (p[s], 0, 0))] + [
        pl.BlockSpec((1, 1, whole, bins), lambda s, m, p, k=k: (k, p[s], 0, 0))
        for k in range(nwin - 1)
    ]
    windows = nwin * win_dev
    return pl.pallas_call(
        functools.partial(
            tiles_kernel, nwin=nwin, win_dev=win_dev, first_rows=first_rows, width=width
        ),
        grid_spec=pltpu.PrefetchScalarGridSpec(
            num_scalar_prefetch=2,
            grid=(slots,),
            in_specs=first_specs + second_specs,
            out_specs=pl.BlockSpec(
                (2, 1, first_rows, width, bins), lambda s, m, p: (0, s, 0, 0, 0)
            ),
            scratch_shapes=[
                pltpu.VMEM((bins // 128, 3 * windows, first_rows, 128), jnp.float32),
                pltpu.VMEM((3 * windows, width, bins), jnp.float32),
            ],
        ),
        out_shape=jax.ShapeDtypeStruct(shape, jnp.bfloat16),
        compiler_params=pltpu.CompilerParams(vmem_limit_bytes=48 * MIB),
        cost_estimate=pl.CostEstimate(
            flops=16 * windows * math.prod(shape), bytes_accessed=12 * MIB, transcendentals=0
        ),
    )(meta, pick, first_in, *[first_x] * (nwin - 1), second_in, *[second_x] * (nwin - 1))


def shards(table, traces, block_members, pair_blocks, pair_owner):
    width = block_members.shape[1]
    local_rows, win_dev, samples = traces.shape
    owners = lax.axis_size("blk")
    nwin = lax.axis_size("win")
    slots = 2 * PAIR_DEV
    meta = jnp.stack([lax.axis_index(name) for name in ("blk", "frq", "win")]).astype(jnp.int32)
    spill, first_send, second_local, mask, pick = spectra(
        meta,
        pair_blocks.reshape(-1),
        pair_owner.reshape(-1),
        block_members,
        traces.reshape(local_rows * win_dev, samples),
        table,
        owners,
        nwin,
        win_dev,
        slots,
    )
    arrived = exchange(spill, first_send, second_local, mask)
    return tiles(meta, pick, *arrived, slots, win_dev, width)


def solution(mesh):
    placed = (
        P(("parts", "blk"), "win", None),
        P(("parts", "blk"), None),
        P("parts", None),
        P("parts", None),
    )

    def whole(traces, block_members, pair_blocks, pair_owner):
        table = jnp.asarray(dft_tables(traces.shape[2], mesh.shape["frq"]))
        return jax.shard_map(
            shards,
            mesh=mesh,
            in_specs=(P(None, None, None),) + placed,
            out_specs=P(None, ("parts", "blk"), "win", None, "frq"),
            check_vma=False,
        )(table, traces, block_members, pair_blocks, pair_owner)

    return whole
```

profile of v0, /device:TPU:0, one launch (start us, length us, event | category | flops | bytes accessed | tf_op | source)
XLA Modules:
  0.0 59.8 jit_solution(10383070708917394964)
XLA Ops:
  0.0 0.0 copy-start.1
  0.0 0.0 copy-start
  0.0 0.1 pad_add_fusion.meta_ref
  0.1 0.8 %copy.7 = s32[8,2]{1,0:T(8,128)S(1)} copy(s32[8,2]{0,1:T(2,128)} %param.7) | data formatting | bytes 128 | tf_op args[2]
  0.8 0.1 reshape.9.blocks_ref
  0.9 2.7 %reshape.11.x_ref = bf16[512,2048]{1,0:T(8,128)(2,1)S(1)} reshape(bf16[256,2,2048]{2,1,0:T(2,128)(2,1)} %param.5) | data formatting | bytes 4194304 | tf_op jit(solution)/shard_map/reshape | solution.py:446
  3.7 0.0 copy-done.1
  3.7 0.0 copy-done
  3.7 6.0 %shard_map.55 = (bf16[2,256,256]{2,1,0:T(8,128)(2,1)S(1)}, bf16[4,2,128,256]{3,2,1,0:T(8,128)(2,1)S(1)}, bf16[4,256,256]{2,1,0:T(8,128)(2,1)S(1)}, f32[4,2,256]{2,1,0:T(2,128)S(1)}, s32[8]{0:T(128)S(1)}) custom-call(s32[3]{0:T(128)S(1)} %pad_add_fusion.meta_ref, s32[16]{0:T(128)S(1)} %reshape.9.blocks_ref, s32[8]{0:T(128)S(1)} %bitcast.4, ...), custom_call_target="tpu_custom_call" | custom-call | flops 1073741824 | bytes 8388608 | tf_op jit(solution)/shard_map/pallas_call | solution.py:152
  9.7 39.5 %shard_map.56 = (bf16[4,2,128,256]{3,2,1,0:T(8,128)(2,1)S(1)}, bf16[4,256,256]{2,1,0:T(8,128)(2,1)S(1)}, bf16[1,4,128,256]{3,2,1,0:T(8,128)(2,1)S(1)}, bf16[1,4,256,256]{3,2,1,0:T(8,128)(2,1)S(1)}) custom-call(bf16[2,256,256]{2,1,0:T(8,128)(2,1)S(1)} %get-tuple-element.15.spill, bf16[4,2,128,256]{3,2,1,0:T(8,128)(2,1)S(1)} %get-tuple-element.16.first_send, ...), custom_call_target="tpu_custom_call" | custom-call | bytes 4194304 | tf_op jit(solution)/shard_map/pallas_call | solution.py:299
  49.2 10.6 %shard_map.57 = bf16[2,4,32,64,256]{4,3,2,1,0:T(8,128)(2,1)} custom-call(s32[3]{0:T(128)S(1)} %pad_add_fusion.meta_ref, s32[8]{0:T(128)S(1)} %get-tuple-element.14.pick_ref, bf16[4,2,128,256]{3,2,1,0:T(8,128)(2,1)S(1)} %get-tuple-element.19.refs_0_, bf16[1,4,128,256]{3,2,1,0:T(8,128)(2,1)S(1)} %get-tuple-element.20.refs_1_, ...), custom_call_target="tpu_custom_call" | custom-call | flops 268435456 | bytes 12582912 | tf_op jit(solution)/shard_map/pallas_call | solution.py:410
Async XLA Ops:
  0.0 3.7 %copy-start.1 = (s32[8,1]{0,1:T(1,128)S(1)}, s32[8,1]{0,1:T(1,128)}, u32[]{:S(2)}) copy-start(s32[8,1]{0,1:T(1,128)} %param.8) | copy-start | bytes 100
  0.0 3.7 %copy-start = (s32[4,64]{1,0:T(4,128)S(1)}, s32[4,64]{1,0:T(4,128)}, u32[]{:S(2)}) copy-start(s32[4,64]{1,0:T(4,128)} %members_ref.1) | copy-start | bytes 3076
where the time goes:
time: 60 us; the launch traced here: 59.8 us
  Pallas kernels  56.1 us (94%)
  local copies, waits for them, and re-layouts  3.59 us (6%)
    pallas_call x1, Pallas kernels, exchange(): pl.pallas_call(functools.partial(exchange_kernel, n, nwin), in_specs=[hbm...  39.5 us
    pallas_call x1, Pallas kernels, tiles(): pl.pallas_call(functools.partial(tiles_kernel, nwin=nwin, win_dev=win_dev...  10.6 us
    pallas_call x1, Pallas kernels, spectra(): pl.pallas_call(functools.partial(spectra_kernel, row_tile=row_tile, win_d...  6 us
    reshape x1, local copies, waits for them, and re-layouts, shards(): traces.reshape(local_rows * win_dev, samples)  2.75 us

commit v1 on v0

--- a/solution.py
+++ b/solution.py
@@ -136,7 +136,7 @@
     bins = cols // 2
     block_count, width = members.shape
     chunk = win_dev * width
-    row_tile = rows // 2
+    row_tile = rows // 4
     whole = 2 * chunk
     shapes = [
         jax.ShapeDtypeStruct((PAIR_DEV, whole, bins), jnp.bfloat16),
@@ -237,7 +237,7 @@
         )
 
     order = sorted(range(1, n), key=lambda d: min(d, n - d))
-    for d in order:
+    for d in order[::-1]:
         first_to(d).start()
     own_first = pltpu.make_async_copy(first_send.at[me], first_out.at[me], own_sems.at[0])
     own_first.start()
@@ -252,7 +252,7 @@
     def _():
         to_left.wait_recv()
 
-    for d in order + [0]:
+    for d in order[::-1] + [0]:
         o = lax.rem(me + d, n)
         total = second_local[o].astype(jnp.float32)
         for q in range(pairs_dev):

time: 60 us -> 60.2 us (level)
  the two profiles are of different devices: /device:TPU:0 before, /device:TPU:8 now
where the time goes in v1:
time: 60.2 us; the launch traced here: 60 us
  Pallas kernels  56.3 us (94%)
  local copies, waits for them, and re-layouts  3.59 us (6%)
    pallas_call x1, Pallas kernels, exchange(): pl.pallas_call(functools.partial(exchange_kernel, n, nwin), in_specs=[hbm...  39.2 us
    pallas_call x1, Pallas kernels, tiles(): pl.pallas_call(functools.partial(tiles_kernel, nwin=nwin, win_dev=win_dev...  10.6 us
    pallas_call x1, Pallas kernels, spectra(): pl.pallas_call(functools.partial(spectra_kernel, row_tile=row_tile, win_d...  6.54 us
    reshape x1, local copies, waits for them, and re-layouts, shards(): traces.reshape(local_rows * win_dev, samples)  2.75 us

profile of v1, /device:TPU:8, one launch (start us, length us, event | category | flops | bytes accessed | tf_op | source)
XLA Modules:
  0.0 60.0 jit_solution(958560707263427037)
XLA Ops:
  0.0 0.0 copy-start.1
  0.0 0.0 copy-start
  0.0 0.1 pad_add_fusion.meta_ref
  0.1 0.8 %copy.7 = s32[8,2]{1,0:T(8,128)S(1)} copy(s32[8,2]{0,1:T(2,128)} %param.7) | data formatting | bytes 128 | tf_op args[2]
  0.8 0.1 reshape.9.blocks_ref
  0.9 2.7 %reshape.11.x_ref = bf16[512,2048]{1,0:T(8,128)(2,1)S(1)} reshape(bf16[256,2,2048]{2,1,0:T(2,128)(2,1)} %param.5) | data formatting | bytes 4194304 | tf_op jit(solution)/shard_map/reshape | solution.py:446
  3.7 0.0 copy-done.1
  3.7 0.0 copy-done
  3.7 6.5 %shard_map.55 = (bf16[2,256,256]{2,1,0:T(8,128)(2,1)S(1)}, bf16[4,2,128,256]{3,2,1,0:T(8,128)(2,1)S(1)}, bf16[4,256,256]{2,1,0:T(8,128)(2,1)S(1)}, f32[4,2,256]{2,1,0:T(2,128)S(1)}, s32[8]{0:T(128)S(1)}) custom-call(s32[3]{0:T(128)S(1)} %pad_add_fusion.meta_ref, s32[16]{0:T(128)S(1)} %reshape.9.blocks_ref, s32[8]{0:T(128)S(1)} %bitcast.4, ...), custom_call_target="tpu_custom_call" | custom-call | flops 1073741824 | bytes 8388608 | tf_op jit(solution)/shard_map/pallas_call | solution.py:152
  10.2 39.2 %shard_map.56 = (bf16[4,2,128,256]{3,2,1,0:T(8,128)(2,1)S(1)}, bf16[4,256,256]{2,1,0:T(8,128)(2,1)S(1)}, bf16[1,4,128,256]{3,2,1,0:T(8,128)(2,1)S(1)}, bf16[1,4,256,256]{3,2,1,0:T(8,128)(2,1)S(1)}) custom-call(bf16[2,256,256]{2,1,0:T(8,128)(2,1)S(1)} %get-tuple-element.15.spill, bf16[4,2,128,256]{3,2,1,0:T(8,128)(2,1)S(1)} %get-tuple-element.16.first_send, ...), custom_call_target="tpu_custom_call" | custom-call | bytes 4194304 | tf_op jit(solution)/shard_map/pallas_call | solution.py:299
  49.4 10.6 %shard_map.57 = bf16[2,4,32,64,256]{4,3,2,1,0:T(8,128)(2,1)} custom-call(s32[3]{0:T(128)S(1)} %pad_add_fusion.meta_ref, s32[8]{0:T(128)S(1)} %get-tuple-element.14.pick_ref, bf16[4,2,128,256]{3,2,1,0:T(8,128)(2,1)S(1)} %get-tuple-element.19.refs_0_, bf16[1,4,128,256]{3,2,1,0:T(8,128)(2,1)S(1)} %get-tuple-element.20.refs_1_, ...), custom_call_target="tpu_custom_call" | custom-call | flops 268435456 | bytes 12582912 | tf_op jit(solution)/shard_map/pallas_call | solution.py:410
Async XLA Ops:
  0.0 3.7 %copy-start.1 = (s32[8,1]{0,1:T(1,128)S(1)}, s32[8,1]{0,1:T(1,128)}, u32[]{:S(2)}) copy-start(s32[8,1]{0,1:T(1,128)} %param.8) | copy-start | bytes 100
  0.0 3.7 %copy-start = (s32[4,64]{1,0:T(4,128)S(1)}, s32[4,64]{1,0:T(4,128)}, u32[]{:S(2)}) copy-start(s32[4,64]{1,0:T(4,128)} %members_ref.1) | copy-start | bytes 3076
